TPU v7x, 32 devices: a whole 2x2x4 slice. The times are simulated.
32 devices in a mesh: row: 4 (over z), col: 8 (over y, x, core).
Axes of the slice: x: 2, y: 2, z: 4, core: 2. Of those that a mesh axis runs over, the one named last changes fastest.
Arguments:
- trailing: bfloat16 [8192, 12288], P('row', 'col'), may hold values from -6 to 6
- low_factor: bfloat16 [2, 8192, 512], P(None, ('row', 'col')), may hold values from -0.1875 to 0.1875
- panel_tops: bfloat16 [2, 512, 12288], P(None, 'row', 'col'), may hold values from -6 to 6
- diag_inverses: bfloat16 [2, 512, 512], replicated, as said below
- link_rows: bfloat16 [512, 512], replicated, may hold values from -0.25 to 0.25
- pivots: int32 [2, 512], replicated, may hold values from 0 to 511, each once within a row
- residual: float32 [1024, 4096], P('row', 'col'), may hold values from -6 to 6
- diagonal: float32 [1024, 4096], P('row', 'col'), may hold values from 0.5 to 2
- coupling: float32 [1024, 4096], P('row', 'col'), may hold values from 0.6 to 1
- basis_cells: int32 [32, 32, 128], P(('row', 'col')), may hold values from 0 to 131071
- basis_weights: float32 [32, 32, 128], P(('row', 'col')), may hold values from 0.1 to 0.4
- coarse_slots: int32 [32, 32, 128], P(('row', 'col')), may hold values from -1 to 383, as said below
Outputs:
- updated: bfloat16 [8192, 12288], P('row', 'col')
- upper_rows: bfloat16 [2, 512, 12288], P(None, None, 'col')
- smoothed: float32 [1024, 4096], P('row', 'col')
- coarse_residual: float32 [12288], P(('row', 'col'))
Inputs may be any that keep to these rules, and one draw needn't show every extreme that they name: `coarse_slots`: -1 marks a padded slot. In every block of 128 slots the live slots come first and number at least 32; in every owner's list one source's block is full. Each diag_inverses[p] is unit lower triangular. Each row of pivots is a permutation.
All inputs are finite; a program needn't handle non-finite values.
Results may differ from a plain program's by a relative error of at most 0.0053.
Values may be sent and summed in bfloat16 or wider, within the bound.
A program may use at most 128 MiB of HBM per device.

v0:
```python
import math

import jax
import jax.numpy as jnp
from jax import lax
from jax.sharding import PartitionSpec as P

MARGIN = 3
SWEEPS = 3
COARSE_DEV = 384


def with_halo(cells, sides, width):
    for axis, dim in sides:
        count = lax.axis_size(axis)
        ends = count - 1
        head = lax.slice_in_dim(cells, 0, width, axis=dim)
        tail = lax.slice_in_dim(cells, cells.shape[dim] - width, cells.shape[dim], axis=dim)
        cells = jnp.concatenate(
            [
                lax.ppermute(tail, axis, [(i, (i + 1) % count) for i in range(ends)]),
                cells,
                lax.ppermute(head, axis, [((i + 1) % count, i) for i in range(ends)]),
            ],
            axis=dim,
        )
    return cells


def sweeps(residual, inverse, coupling):
    source = residual * inverse
    weight = 0.25 * coupling
    solution = source
    for sweep_number in range(SWEEPS - 1):
        padded = jnp.pad(solution, 1)
        beside = padded[2:, 1:-1] + padded[:-2, 1:-1] + padded[1:-1, 2:] + padded[1:-1, :-2]
        solution = source + weight * beside
    return solution


def ordered_inverse(inverse, order):
    count = order.shape[0]
    columns = lax.broadcasted_iota(jnp.int32, (count, count), 1)
    permuter = (order[:, None] == columns).astype(jnp.bfloat16)
    return jnp.dot(inverse, permuter, preferred_element_type=jnp.float32).astype(jnp.bfloat16)


def solve_panels(top_rows, diag_inverses, link_rows, pivots):
    first_map = ordered_inverse(diag_inverses[0], pivots[0])
    second_map = ordered_inverse(diag_inverses[1], pivots[1])
    upper_one = jnp.dot(first_map, top_rows[0], preferred_element_type=jnp.float32).astype(
        jnp.bfloat16
    )
    panel_two = (
        top_rows[1].astype(jnp.float32)
        - jnp.dot(link_rows, upper_one, preferred_element_type=jnp.float32)
    ).astype(jnp.bfloat16)
    upper_two = jnp.dot(second_map, panel_two, preferred_element_type=jnp.float32).astype(
        jnp.bfloat16
    )
    return jnp.stack([upper_one, upper_two])


def shards(
    trailing,
    low_factor,
    panel_tops,
    diag_inverses,
    link_rows,
    pivots,
    residual,
    diagonal,
    coupling,
    basis_cells,
    basis_weights,
    coarse_slots,
):
    cells_x, cells_y = residual.shape
    flat_cells = basis_cells[0].reshape(-1)
    total_slots = flat_cells.shape[0]
    block_width = math.gcd(total_slots, 2048)
    row_index = (flat_cells // cells_y).reshape(-1, block_width)
    col_index = (flat_cells % cells_y).reshape(-1, block_width)
    row_iota = lax.broadcasted_iota(jnp.int32, (1, cells_x), 1)
    col_iota = lax.broadcasted_iota(jnp.int32, (1, cells_y), 1)

    def pick_cells(pair):
        rows_here, cols_here = pair
        selector = (rows_here[:, None] == row_iota).astype(jnp.float32)
        picked = jnp.dot(
            selector, residual, precision=lax.Precision.HIGHEST, preferred_element_type=jnp.float32
        )
        return jnp.sum(jnp.where(cols_here[:, None] == col_iota, picked, 0.0), axis=1)

    gathered = lax.map(pick_cells, (row_index, col_index)).reshape(basis_weights[0].shape)
    outgoing = gathered * basis_weights[0]
    arrived = lax.all_to_all(outgoing, ("row", "col"), split_axis=0, concat_axis=0, tiled=True)
    owner_iota = lax.broadcasted_iota(jnp.int32, (1, COARSE_DEV), 1)
    owned_slots = coarse_slots[0].reshape(-1, block_width)
    arrived_blocks = arrived.reshape(-1, block_width)

    def add_block(pair):
        slots_here, values_here = pair
        selector = (slots_here[:, None] == owner_iota).astype(jnp.float32)
        return jnp.dot(
            values_here[None, :],
            selector,
            precision=lax.Precision.HIGHEST,
            preferred_element_type=jnp.float32,
        )[0]

    coarse_residual = jnp.sum(lax.map(add_block, (owned_slots, arrived_blocks)), axis=0)
    stacked = jnp.stack([residual, diagonal, coupling])
    extended = with_halo(stacked, (("row", 1), ("col", 2)), MARGIN)
    along_x = (
        lax.axis_index("row") * cells_x
        - MARGIN
        + lax.broadcasted_iota(jnp.int32, (cells_x + 2 * MARGIN, 1), 0)
    )
    along_y = (
        lax.axis_index("col") * cells_y
        - MARGIN
        + lax.broadcasted_iota(jnp.int32, (1, cells_y + 2 * MARGIN), 1)
    )
    inside = (
        (along_x >= 0)
        & (along_x < cells_x * lax.axis_size("row"))
        & (along_y >= 0)
        & (along_y < cells_y * lax.axis_size("col"))
    )
    inverse = 1.0 / jnp.where(inside, extended[1], 1.0)
    solution = sweeps(extended[0], inverse, extended[2])
    smoothed = solution[MARGIN : MARGIN + cells_x, MARGIN : MARGIN + cells_y]
    whole_tops = lax.all_gather(panel_tops, "row", axis=1, tiled=True)
    upper_rows = solve_panels(whole_tops, diag_inverses, link_rows, pivots)
    pieces = lax.all_gather(low_factor, "col", axis=1, tiled=True)
    total = (
        trailing.astype(jnp.float32)
        - jnp.dot(pieces[0], upper_rows[0], preferred_element_type=jnp.float32)
        - jnp.dot(pieces[1], upper_rows[1], preferred_element_type=jnp.float32)
    )
    updated = total.astype(jnp.bfloat16)
    return (updated, upper_rows, smoothed, coarse_residual)


def solution(mesh):
    return jax.shard_map(
        shards,
        mesh=mesh,
        in_specs=(
            P("row", "col"),
            P(None, ("row", "col"), None),
            P(None, "row", "col"),
            P(),
            P(),
            P(),
            P("row", "col"),
            P("row", "col"),
            P("row", "col"),
            P(("row", "col"), None, None),
            P(("row", "col"), None, None),
            P(("row", "col"), None, None),
        ),
        out_specs=(P("row", "col"), P(None, None, "col"), P("row", "col"), P(("row", "col"))),
        check_vma=False,
    )
```

profile of v0, /device:TPU:1, one launch (start us, length us, event | category | flops | bytes accessed | tf_op | source)
XLA Modules:
  0.0 146.9 jit_solution(6126488427347177308)
XLA Ops:
  7.2 0.0 copy-start
  7.2 0.0 copy-start.3
  7.2 0.0 copy-start.6
  7.2 0.0 all-gather.3.cloned.1.call-start
  7.2 0.7 all-gather.3.cloned.1.call-update
  7.9 0.0 all-gather.5.cloned.1.call-start
  8.0 0.7 all-gather.5.cloned.1.call-update
  8.7 0.8 pad_maximum_fusion.9
  9.5 4.0 %collective-permute-start = (f32[3,3,512]{2,1,0:T(4,128)S(1)}, f32[3,3,512]{2,1,0:T(4,128)S(1)}, u32[]{:S(2)}, u32[]{:S(2)}) collective-permute-start(f32[3,3,512]{2,1,0:T(4,128)S(1)} %get-tuple-element.123), channel_id=1, source_target_pairs={{0,8},{8,16},{16,24},{1,9},{9,17},{17,25},{2,10},{10,18},{18,26},{... | collective-permute-start | bytes 55304 | tf_op jit(solution)/shard_map/ppermute | solution.py:21
  13.5 1.3 collective-permute-start.1
  14.9 0.0 copy-done.6
  14.9 0.1 and_select_fusion
  14.9 0.0 copy-done.3
  15.0 0.0 copy-start.5
  15.0 0.0 copy-start.8
  15.0 0.0 copy-start.1
  15.0 0.0 copy-start.2
  15.0 6.0 %while.22 = (s32[]{:T(128)}, f32[2,2048]{1,0:T(2,128)S(1)}, s32[2,2048]{1,0:T(2,128)S(1)}, s32[2,2048]{1,0:T(2,128)S(1)}, f32[256,512]{1,0:T(8,128)S(1)}, /*index=5*/s32[]{:T(128)}, s32[]{:T(128)}) while((s32[]{:T(128)}, f32[2,2048]{1,0:T(2,128)S(1)}, s32[2,2048]{1,0:T(2,128)S(1)}, s32[2,2048]{1,0:T(2,128)S(1)}, ...), condition=%wide.region_2.3_spmd.clone, body=%wide.region_0.2_spmd.clone.sunk | while | flops 3224893440 | bytes 598101 | solution.py:95
  15.0 2.9 %select_reduce_fusion.2 = f32[2048]{0:T(1024)S(1)} fusion(f32[256,512]{1,0:T(8,128)S(1)} %get-tuple-element.213, s32[2048]{0:T(1024)S(1)} %bitcast.100, s32[2048]{0:T(1024)S(1)} %bitcast.99), kind=kOutput, calls=%fused_computation.4.clone.1 | convolution fusion | flops 3224893440 | bytes 548864 | tf_op jit(solution)/shard_map/while/body/eval_jaxpr/dot_general | solution.py:90
  17.9 0.1 dynamic_update_slice.12
  18.1 2.9 %select_reduce_fusion.2 = f32[2048]{0:T(1024)S(1)} fusion(f32[256,512]{1,0:T(8,128)S(1)} %get-tuple-element.213, s32[2048]{0:T(1024)S(1)} %bitcast.100, s32[2048]{0:T(1024)S(1)} %bitcast.99), kind=kOutput, calls=%fused_computation.4.clone.1 | convolution fusion | flops 3224893440 | bytes 548864 | tf_op jit(solution)/shard_map/while/body/eval_jaxpr/dot_general | solution.py:90
  20.9 0.1 dynamic_update_slice.12
  21.1 0.0 copy-done.5
  21.1 0.6 mul.42
  21.7 7.6 %all-to-all-start = ((f32[32,1,128]{2,1,0:T(1,128)}), f32[32,1,128]{2,1,0:T(1,128)S(1)}, u32[]{:S(2)}, u32[]{:S(2)}) async-start(f32[32,1,128]{2,1,0:T(1,128)} %mul.42), calls=%async_computation | async-start | bytes 32768 | tf_op jit(solution)/shard_map/all_to_all | solution.py:97
  29.3 0.0 copy-done.8
  29.4 0.0 collective-permute-done
  29.4 0.0 collective-permute-done.1
  29.4 0.0 copy-done.1
  29.4 0.0 copy-done.2
  29.4 1.0 pad_maximum_fusion.6
  30.4 3.5 %collective-permute-start.2 = (f32[3,262,3]{2,1,0:T(8,128)}, f32[3,262,3]{2,1,0:T(8,128)S(1)}, u32[]{:S(2)}, u32[]{:S(2)}) collective-permute-start(f32[3,262,3]{2,1,0:T(8,128)} %get-tuple-element.121), channel_id=1, source_target_pairs={{0,1},{1,2},{2,3},{3,4},{4,5},{5,6},{6,7},{8,9},{9,10},{10,11},{11... | collective-permute-start | bytes 28304 | tf_op jit(solution)/shard_map/ppermute | solution.py:21
  33.9 2.1 %collective-permute-start.3 = (f32[3,262,3]{2,1,0:T(8,128)S(1)}, f32[3,262,3]{2,1,0:T(8,128)S(1)}, u32[]{:S(2)}, u32[]{:S(2)}) collective-permute-start(f32[3,262,3]{2,1,0:T(8,128)S(1)} %get-tuple-element.122), channel_id=1, source_target_pairs={{1,0},{2,1},{3,2},{4,3},{5,4},{6,5},{7,6},{9,8},{10,9},{11,10},{12... | collective-permute-start | bytes 28304 | tf_op jit(solution)/shard_map/ppermute | solution.py:23
  36.0 0.0 copy-start.7
  36.0 8.6 %copy.18 = bf16[2048,1536]{0,1:T(8,128)(2,1)} copy(bf16[2048,1536]{1,0:T(8,128)(2,1)} %param.16) | data formatting | bytes 12582912 | tf_op args[0]
  44.7 0.0 copy-done.7
  44.7 0.0 collective-permute-done.2
  44.7 0.6 collective-permute-done.3
  45.3 0.8 pad_maximum_fusion.1
  46.1 0.2 fusion.21
  46.3 0.4 multiply_add_fusion
  46.7 0.4 pad_slice_fusion.5
  47.3 1.9 %slice_add_fusion = f32[256,512]{1,0:T(8,128)} fusion(f32[262,518]{1,0:T(8,128)S(1)} %fusion.21, f32[262,518]{1,0:T(8,128)S(1)} %fusion.18, f32[262,518]{1,0:T(8,128)S(1)} %get-tuple-element.128, f32[262,518]{1,0:T(8,128)S(1)} %get-tuple-element.127, f32[262,518]{1,0:T(8,128)S(1)} %get-tuple-element.126, f32[262,518]{1,0:T(8,128)S(1)} %get-tuple-element.125), kind=kLoop, calls=%fused_computation.52 | loop fusion | flops 655360 | bytes 3670016 | tf_op jit(solution)/shard_map/add | solution.py:37
  49.2 0.0 all-to-all-done
  49.2 0.5 broadcast.86
  49.7 0.7 reduce.3
  50.4 2.5 %while.23 = (s32[]{:T(128)}, f32[2,384]{1,0:T(2,128)S(1)}, f32[2,2048]{1,0:T(2,128)S(1)}, s32[2,2048]{1,0:T(2,128)S(1)}, s32[]{:T(128)}, /*index=5*/s32[]{:T(128)}) while((s32[]{:T(128)}, f32[2,384]{1,0:T(2,128)S(1)}, f32[2,2048]{1,0:T(2,128)S(1)}, s32[2,2048]{1,0:T(2,128)S(1)}, s32[]{:T(128)}, /*index=5*/s32[]{:T(128)}) %tuple.57), condition=%wide.region_4.5_spmd.clone, body=%wide.region_3.4_spmd.clone.sunk | while | flops 10223618 | bytes 37457 | solution.py:112
  50.4 1.2 fusion.56
  51.7 1.2 fusion.56
  52.9 0.6 reduce_sum.18
  53.5 22.0 %all-gather.3.cloned.1.call-done = bf16[2,512,1536]{2,1,0:T(8,128)(2,1)} async-done(((bf16[2,128,1536]{2,1,0:T(8,128)(2,1)}), bf16[2,512,1536]{2,1,0:T(8,128)(2,1)}) %all-gather.3.cloned.1.call-update) | async-done | bytes 3145744 | tf_op jit(solution)/shard_map/all_gather | solution.py:134
  75.5 3.1 %convolution_convert_fusion.1 = bf16[512,1536]{1,0:T(8,128)(2,1)S(1)} fusion(bf16[2,512,1536]{2,1,0:T(8,128)(2,1)} %all-gather.3.cloned.1.call-done, bf16[2,512,512]{2,1,0:T(8,128)(2,1)} %param.19, s32[512]{0:T(512)S(1)} %bitcast.103), kind=kOutput, calls=%fused_computation.23 | convolution fusion | flops 1075314688 | bytes 3672064 | tf_op jit(solution)/shard_map/dot_general | solution.py:51
  78.6 0.0 copy-done
  78.7 3.5 %fusion.14 = bf16[512,1536]{1,0:T(8,128)(2,1)} fusion(bf16[512,512]{1,0:T(8,128)(2,1)S(1)} %copy-done, bf16[512,1536]{1,0:T(8,128)(2,1)S(1)} %convolution_convert_fusion.1, bf16[2,512,1536]{2,1,0:T(8,128)(2,1)} %all-gather.3.cloned.1.call-done), kind=kOutput, calls=%fused_computation.24 | convolution fusion | flops 807665664 | bytes 5242880 | tf_op jit(solution)/shard_map/dot_general | solution.py:56
  82.2 4.4 %convolution_convert_fusion = bf16[512,1536]{1,0:T(8,128)(2,1)} fusion(bf16[512,1536]{1,0:T(8,128)(2,1)} %fusion.14, bf16[2,512,512]{2,1,0:T(8,128)(2,1)} %param.19, s32[512]{0:T(512)S(1)} %bitcast.102), kind=kOutput, calls=%fused_computation.22 | convolution fusion | flops 1075314688 | bytes 3672064 | tf_op jit(solution)/shard_map/dot_general | solution.py:58
  86.6 3.4 %pad_maximum_fusion = bf16[2,512,1536]{2,1,0:T(8,128)(2,1)} fusion(bf16[1,512,1536]{2,1,0:T(8,128)(2,1)} %bitcast.96, bf16[1,512,1536]{2,1,0:T(8,128)(2,1)S(1)} %bitcast.95), kind=kLoop, calls=%fused_computation.21 | loop fusion | flops 1572864 | bytes 6291456 | tf_op jit(solution)/shard_map/stack | solution.py:61
  89.9 23.2 %all-gather.5.cloned.1.call-done = bf16[2,2048,512]{2,1,0:T(8,128)(2,1)} async-done(((bf16[2,256,512]{2,1,0:T(8,128)(2,1)}), bf16[2,2048,512]{2,1,0:T(8,128)(2,1)}) %all-gather.5.cloned.1.call-update) | async-done | bytes 4194320 | tf_op jit(solution)/shard_map/all_gather | solution.py:136
  113.2 0.0 copy-start.4
  113.2 0.0 copy-start.9
  113.2 8.1 %fusion.15 = f32[1536,2048]{1,0:T(8,128)} fusion(bf16[512,1536]{1,0:T(8,128)(2,1)S(1)} %convolution_convert_fusion.1, bf16[2,2048,512]{2,1,0:T(8,128)(2,1)} %all-gather.5.cloned.1.call-done), kind=kOutput, calls=%fused_computation.27 | convolution fusion | flops 3221225472 | bytes 16252928 | tf_op jit(solution)/shard_map/dot_general | solution.py:139
  121.3 0.0 copy-done.4
  121.3 0.0 copy-done.9
  121.3 10.1 %fusion.12 = bf16[2048,1536]{0,1:T(8,128)(2,1)} fusion(f32[1536,2048]{1,0:T(8,128)} %fusion.15, bf16[2048,1536]{0,1:T(8,128)(2,1)} %copy.18, bf16[512,1536]{1,0:T(8,128)(2,1)S(1)} %copy-done.4, bf16[2,2048,512]{2,1,0:T(8,128)(2,1)S(1)} %copy-done.9), kind=kOutput, calls=%fused_computation.17 | convolution fusion | flops 3233808384 | bytes 28835840 | tf_op jit(solution)/shard_map/dot_general | solution.py:140
  131.4 8.6 %copy.19 = bf16[2048,1536]{1,0:T(8,128)(2,1)} copy(bf16[2048,1536]{0,1:T(8,128)(2,1)} %fusion.12) | data formatting | bytes 12582912
  (16 shorter events, 0.3 us)
Async XLA Ops:
  7.2 71.5 %copy-start = (bf16[512,512]{1,0:T(8,128)(2,1)S(1)}, bf16[512,512]{1,0:T(8,128)(2,1)}, u32[]{:S(2)}) copy-start(bf16[512,512]{1,0:T(8,128)(2,1)} %param.20) | copy-start | bytes 1572868
  7.2 7.8 %copy-start.3 = (f32[256,512]{1,0:T(8,128)S(1)}, f32[256,512]{1,0:T(8,128)}, u32[]{:S(2)}) copy-start(f32[256,512]{1,0:T(8,128)} %param.22) | copy-start | bytes 1572868
  7.2 7.7 %copy-start.6 = (s32[1,32,128]{2,1,0:T(8,128)S(1)}, s32[1,32,128]{2,1,0:T(8,128)}, u32[]{:S(2)}) copy-start(s32[1,32,128]{2,1,0:T(8,128)} %param.25) | copy-start | bytes 49156
  7.2 68.3 %all-gather.3.cloned.1.call-start = ((), (), s32[]{:S(2)}) async-start(), calls=%async_computation.1 | async-start | bytes 3932160 | tf_op jit(solution)/shard_map/all_gather | solution.py:134
  7.9 105.2 %all-gather.5.cloned.1.call-start = ((), (), s32[]{:S(2)}) async-start(), calls=%async_computation.2 | async-start | bytes 4718592 | tf_op jit(solution)/shard_map/all_gather | solution.py:136
  9.5 19.9 %collective-permute-start = (f32[3,3,512]{2,1,0:T(4,128)S(1)}, f32[3,3,512]{2,1,0:T(4,128)S(1)}, u32[]{:S(2)}, u32[]{:S(2)}) collective-permute-start(f32[3,3,512]{2,1,0:T(4,128)S(1)} %get-tuple-element.123), channel_id=1, source_target_pairs={{0,8},{8,16},{16,24},{1,9},{9,17},{17,25},{2,10},{10,18},{18,26},{... | collective-permute-start | bytes 55304 | tf_op jit(solution)/shard_map/ppermute | solution.py:21
  13.5 15.8 %collective-permute-start.1 = (f32[3,3,512]{2,1,0:T(4,128)S(1)}, f32[3,3,512]{2,1,0:T(4,128)S(1)}, u32[]{:S(2)}, u32[]{:S(2)}) collective-permute-start(f32[3,3,512]{2,1,0:T(4,128)S(1)} %get-tuple-element.124), channel_id=1, source_target_pairs={{8,0},{16,8},{24,16},{9,1},{17,9},{25,17},{10,2},{18,10},{26,18},{... | collective-permute-start | bytes 55304 | tf_op jit(solution)/shard_map/ppermute | solution.py:23
  15.0 6.1 %copy-start.5 = (f32[1,32,128]{2,1,0:T(8,128)S(1)}, f32[1,32,128]{2,1,0:T(8,128)}, u32[]{:S(2)}) copy-start(f32[1,32,128]{2,1,0:T(8,128)} %param.26) | copy-start | bytes 49156
  15.0 14.4 %copy-start.8 = (s32[2,512]{1,0:T(2,128)S(1)}, s32[2,512]{1,0:T(2,128)}, u32[]{:S(2)}) copy-start(s32[2,512]{1,0:T(2,128)} %param.21) | copy-start | bytes 12292
  15.0 14.4 %copy-start.1 = (f32[256,512]{1,0:T(8,128)S(1)}, f32[256,512]{1,0:T(8,128)}, u32[]{:S(2)}) copy-start(f32[256,512]{1,0:T(8,128)} %param.24) | copy-start | bytes 1572868
  15.0 14.4 %copy-start.2 = (f32[256,512]{1,0:T(8,128)S(1)}, f32[256,512]{1,0:T(8,128)}, u32[]{:S(2)}) copy-start(f32[256,512]{1,0:T(8,128)} %param.23) | copy-start | bytes 1572868
  21.7 27.5 %all-to-all-start = ((f32[32,1,128]{2,1,0:T(1,128)}), f32[32,1,128]{2,1,0:T(1,128)S(1)}, u32[]{:S(2)}, u32[]{:S(2)}) async-start(f32[32,1,128]{2,1,0:T(1,128)} %mul.42), calls=%async_computation | async-start | bytes 32768 | tf_op jit(solution)/shard_map/all_to_all | solution.py:97
  30.4 14.3 %collective-permute-start.2 = (f32[3,262,3]{2,1,0:T(8,128)}, f32[3,262,3]{2,1,0:T(8,128)S(1)}, u32[]{:S(2)}, u32[]{:S(2)}) collective-permute-start(f32[3,262,3]{2,1,0:T(8,128)} %get-tuple-element.121), channel_id=1, source_target_pairs={{0,1},{1,2},{2,3},{3,4},{4,5},{5,6},{6,7},{8,9},{9,10},{10,11},{11... | collective-permute-start | bytes 28304 | tf_op jit(solution)/shard_map/ppermute | solution.py:21
  33.9 11.4 %collective-permute-start.3 = (f32[3,262,3]{2,1,0:T(8,128)S(1)}, f32[3,262,3]{2,1,0:T(8,128)S(1)}, u32[]{:S(2)}, u32[]{:S(2)}) collective-permute-start(f32[3,262,3]{2,1,0:T(8,128)S(1)} %get-tuple-element.122), channel_id=1, source_target_pairs={{1,0},{2,1},{3,2},{4,3},{5,4},{6,5},{7,6},{9,8},{10,9},{11,10},{12... | collective-permute-start | bytes 28304 | tf_op jit(solution)/shard_map/ppermute | solution.py:23
  36.0 8.7 %copy-start.7 = (s32[1,32,128]{2,1,0:T(8,128)S(1)}, s32[1,32,128]{2,1,0:T(8,128)}, u32[]{:S(2)}) copy-start(s32[1,32,128]{2,1,0:T(8,128)} %param.27) | copy-start | bytes 49156
  113.2 8.1 %copy-start.4 = (bf16[512,1536]{1,0:T(8,128)(2,1)S(1)}, bf16[512,1536]{1,0:T(8,128)(2,1)}, u32[]{:S(2)}) copy-start(bf16[512,1536]{1,0:T(8,128)(2,1)} %convolution_convert_fusion) | copy-start | bytes 4718596
  113.2 8.1 %copy-start.9 = (bf16[2,2048,512]{2,1,0:T(8,128)(2,1)S(1)}, bf16[2,2048,512]{2,1,0:T(8,128)(2,1)}, u32[]{:S(2)}) copy-start(bf16[2,2048,512]{2,1,0:T(8,128)(2,1)} %all-gather.5.cloned.1.call-done) | copy-start | bytes 12582916
Sparse Core Ops, SparseCore 0:
  9.6 65.8 all-gather.2
  77.4 35.6 all-gather.4
where the time goes:
time: 148 us; the launch traced here: 147 us
  waiting for transfers between devices  47.2 us (32%)
  matrix products  37.3 us (25%)
  local copies, waits for them, and re-layouts  18.7 us (13%)
  starting transfers between devices  18.6 us (13%)
  between operations  14.4 us (10%)
  other arithmetic  10.5 us (7%)
    all_gather x1, waiting for transfers between devices, shards(): pieces = lax.all_gather(low_factor, 'col', axis=1, tiled=True)  23.2 us
    all_gather x1, waiting for transfers between devices, shards(): whole_tops = lax.all_gather(panel_tops, 'row', axis=1, tiled=True)  22 us
    unnamed x22, local copies, waits for them, and re-layouts  17.3 us
    dot_general x1, matrix products, shards(): jnp.dot(pieces[1], upper_rows[1], preferred_element_type=jnp.float32)  10.1 us
    dot_general x1, matrix products, shards(): jnp.dot(pieces[0], upper_rows[0], preferred_element_type=jnp.float32)  8.12 us
    all_to_all x1, starting transfers between devices, shards(): lax.all_to_all(outgoing, ('row', 'col'), split_axis=0, concat_axis=0, til...  7.61 us
    ppermute x2, starting transfers between devices, with_halo(): lax.ppermute(tail, axis, [(i, (i + 1) % count) for i in range(ends)])  7.56 us
    dot_general x2, matrix products, pick_cells(): jnp.dot(selector, residual, precision=lax.Precision.HIGHEST, preferred_el...  5.72 us
  transfers between devices with their start and end apart: 7, of which 3 were waited for; matrix products, arithmetic and copies ran while one was open for 27% of the time, Pallas kernels for 0%

commit v1 on v0

v1 whole, which is shorter than its diff:
```python
import functools

import jax
import jax.numpy as jnp
from jax import lax
from jax.experimental import pallas as pl
from jax.experimental.pallas import tpu as pltpu
from jax.sharding import PartitionSpec as P

MARGIN = 3
COARSE_DEV = 384
CHUNK = 256
ROW_TILE = 512
MESH = pl.DeviceIdType.MESH
F32 = jnp.float32
BF16 = jnp.bfloat16


def flipped(index, mask):
    result, bit = index, 1
    while bit <= mask:
        if mask & bit:
            result = result + bit * (1 - 2 * ((index // bit) % 2))
        bit *= 2
    return result


def masks_of(bits):
    masks = [0]
    for bit in bits:
        masks = masks + [m | bit for m in masks]
    return masks


def low_orders(count):
    bits = [1 << i for i in range(count.bit_length() - 1)]
    far, near = bits[1:], bits[:1]
    return (far + near, far[::-1] + near)


def kernel(
    R,
    C,
    trailing,
    low,
    tops,
    inverses,
    link,
    pivots,
    residual,
    diagonal,
    coupling,
    cells,
    weights,
    slots,
    updated,
    upper,
    smoothed,
    coarse,
    tb,
    lb,
    tr,
    up,
    maps,
    S,
    Wt,
    E1,
    hrow,
    hout,
    hcol,
    parts,
    st1,
    r1,
    r2,
    tops_send,
    tops_recv,
    low_send,
    low_recv,
    hrow_send,
    hrow_recv,
    hcol_send,
    hcol_recv,
    a1_send,
    a1_recv,
    a2_send,
    a2_recv,
    load_sem,
    tops_load,
    upd_sem,
    upp_sem,
):
    me_r, me_c = lax.axis_index("row"), lax.axis_index("col")
    chunks = tb.shape[0]
    kb = tops.shape[1]
    own_x, own_y = residual.shape
    owners = cells.shape[0]

    def remote(src, dst, send, recv, row, col):
        return pltpu.make_async_remote_copy(
            src_ref=src,
            dst_ref=dst,
            send_sem=send,
            recv_sem=recv,
            device_id=(row, col),
            device_id_type=MESH,
        )

    barrier = pltpu.get_barrier_semaphore()
    for i in range(1, R):
        pl.semaphore_signal(
            barrier, inc=1, device_id=(lax.rem(me_r + i, R), me_c), device_id_type=MESH
        )
    for i in range(1, C):
        pl.semaphore_signal(
            barrier, inc=1, device_id=(me_r, lax.rem(me_c + i, C)), device_id_type=MESH
        )

    load_trailing = pltpu.make_async_copy(trailing, tr, load_sem.at[0])
    load_low = [
        pltpu.make_async_copy(low.at[p], lb.at[p, me_c], load_sem.at[1 + p]) for p in range(2)
    ]
    load_tops = [
        pltpu.make_async_copy(
            tops.at[:, :, pl.ds(k * CHUNK, CHUNK)],
            tb.at[k, :, pl.ds(pl.multiple_of(me_r * kb, kb), kb), :],
            tops_load.at[k],
        )
        for k in range(chunks)
    ]

    def tops_copy(way, d, k):
        step = 1 if way == 0 else -1
        block = me_r - step * d
        place = tb.at[k, :, pl.ds(pl.multiple_of(block * kb, kb), kb), :]
        src = tops.at[:, :, pl.ds(k * CHUNK, CHUNK)] if d == 0 else place
        return remote(
            src, place, tops_send.at[way, d, k], tops_recv.at[way, d, k], me_r + step, me_c
        )

    def tops_sends(way, d):
        if way == 0:
            return (me_r - d >= 0) & (me_r + 1 < R)
        return (me_r + d < R) & (me_r - 1 >= 0)

    def tops_start(way, d, k):
        @pl.when(tops_sends(way, d))
        def _():
            tops_copy(way, d, k).start()

    def tops_arrive(way, d, k):
        step = 1 if way == 0 else -1
        block = me_r - step * (d + 1)

        @pl.when((block >= 0) & (block < R))
        def _():
            place = tb.at[k, :, pl.ds(pl.multiple_of(block * kb, kb), kb), :]
            remote(
                place, place, tops_send.at[way, d, k], tops_recv.at[way, d, k], me_r, me_c
            ).wait_recv()

    orders = low_orders(C)

    def low_copy(p, m, bit):
        block = flipped(me_c, m)
        place = lb.at[p, block]
        src = low.at[p] if m == 0 else place
        return remote(
            src, place, low_send.at[p, m | bit], low_recv.at[p, m | bit], me_r, flipped(me_c, bit)
        )

    def low_arrive(p, m):
        place = lb.at[p, flipped(me_c, m)]
        remote(place, place, low_send.at[p, m], low_recv.at[p, m], me_r, me_c).wait_recv()

    def low_forward(p, t):
        order = orders[p]
        for m in masks_of(order[:t]):
            arrived = m | order[t]
            low_arrive(p, arrived)
            for bit in order[t + 1 :]:
                low_copy(p, arrived, bit).start()

    pl.semaphore_wait(barrier, R - 1 + C - 1)
    for k in range(chunks):
        for way in range(2):
            tops_start(way, 0, k)
    for t in range(len(orders[0])):
        for p in range(2):
            low_copy(p, 0, orders[p][t]).start()
    for copy in load_tops + load_low:
        copy.start()
    load_trailing.start()

    mid_y = pl.ds(128, own_y)
    src_own = residual[...] * (1.0 / diagonal[...])
    S[pl.ds(16, own_x), mid_y] = src_own
    Wt[pl.ds(16, own_x), mid_y] = 0.25 * coupling[...]
    arrays = (S, Wt)
    last_x = own_x + 8
    for a in range(2):
        hout[0, a] = arrays[a][pl.ds(16, 8), mid_y]
        hout[1, a] = arrays[a][pl.ds(last_x, 8), mid_y]

    def row_copy(side):
        step = -1 if side == 0 else 1
        return remote(
            hout.at[side], hrow.at[1 - side], hrow_send.at[side], hrow_recv.at[1 - side],
            me_r + step, me_c,
        )

    @pl.when(me_r > 0)
    def _():
        row_copy(0).start()

    @pl.when(me_r < R - 1)
    def _():
        row_copy(1).start()

    whole = residual[...]
    high = whole.astype(BF16)
    rest = whole - high.astype(F32)
    middle = rest.astype(BF16)
    parts[pl.ds(0, own_x), :] = high
    parts[pl.ds(own_x, own_x), :] = middle
    parts[pl.ds(2 * own_x, own_x), :] = (rest - middle.astype(F32)).astype(BF16)
    bits_y = own_y.bit_length() - 1

    def pick(i, carry):
        rows = cells[pl.ds(pl.multiple_of(i * 8, 8), 8), :]
        weight = weights[pl.ds(pl.multiple_of(i * 8, 8), 8), :]
        flat = jnp.concatenate([rows[j : j + 1, :] for j in range(8)], axis=1)
        at_x = lax.shift_right_logical(flat, bits_y)
        at_y = flat & (own_y - 1)
        width = flat.shape[1]
        chosen = (lax.broadcasted_iota(jnp.int32, (own_y, width), 0) == at_y).astype(F32)
        picked = jnp.dot(parts[...], chosen.astype(BF16), preferred_element_type=F32)
        column = (
            picked[:own_x] + picked[own_x : 2 * own_x] + picked[2 * own_x : 3 * own_x]
        )
        here = lax.broadcasted_iota(jnp.int32, (own_x, width), 0) == at_x
        values = jnp.sum(jnp.where(here, column, 0.0), axis=0, keepdims=True)
        for j in range(8):
            index = i * 8 + j
            st1[index % C, index // C] = (
                values[:, j * 128 : (j + 1) * 128] * weight[j : j + 1, :]
            )
        return carry

    lax.fori_loop(0, owners // 8, pick, 0)

    def a1_copy(i):
        return remote(
            st1.at[lax.rem(me_c + i, C)], r1.at[me_c], a1_send.at[i], a1_recv.at[i],
            me_r, lax.rem(me_c + i, C),
        )

    for i in range(1, C):
        a1_copy(i).start()
    r1[me_c] = st1[me_c]

    for p in range(2):
        low_forward(p, 0)

    row_at = lax.broadcasted_iota(jnp.int32, (8, own_y), 0)
    edge_zero = jnp.zeros((8, S.shape[1]), F32)
    for a in range(2):
        arrays[a][pl.ds(0, 8), :] = edge_zero
        arrays[a][pl.ds(own_x + 24, 8), :] = edge_zero
    for side in range(2):
        start = 8 if side == 0 else own_x + 16
        keep = row_at >= 8 - MARGIN if side == 0 else row_at < MARGIN
        present = me_r > 0 if side == 0 else me_r < R - 1

        @pl.when(present)
        def _():
            remote(
                hout.at[side], hrow.at[side], hrow_send.at[side], hrow_recv.at[side], me_r, me_c
            ).wait_recv()
            for a in range(2):
                arrays[a][pl.ds(start, 8), mid_y] = jnp.where(keep, hrow[side, a], 0.0)

        @pl.when(jnp.logical_not(present))
        def _():
            for a in range(2):
                arrays[a][pl.ds(start, 8), mid_y] = jnp.zeros((8, own_y), F32)

    tall = own_x + 16
    lane = lax.broadcasted_iota(jnp.int32, (tall, 128), 1)
    left_tile, right_tile = pl.ds(0, 128), pl.ds(128 + own_y, 128)
    first_tile, last_tile = pl.ds(128, 128), pl.ds(own_y, 128)
    span = pl.ds(8, tall)
    hcol[0] = jnp.where(
        lane < MARGIN, S[span, first_tile], pltpu.roll(Wt[span, first_tile], 8, 1)
    )
    hcol[1] = jnp.where(
        lane >= 128 - MARGIN, S[span, last_tile], pltpu.roll(Wt[span, last_tile], 120, 1)
    )

    def col_copy(side):
        step = -1 if side == 0 else 1
        return remote(
            hcol.at[side], hcol.at[3 - side], hcol_send.at[side], hcol_recv.at[1 - side],
            me_r, me_c + step,
        )

    @pl.when(me_c > 0)
    def _():
        col_copy(0).start()

    @pl.when(me_c < C - 1)
    def _():
        col_copy(1).start()

    count = inverses.shape[1]
    for p in range(2):
        permuter = (
            lax.broadcasted_iota(jnp.int32, (count, count), 0) == pivots[p : p + 1, :]
        ).astype(F32).astype(BF16)
        maps[p] = lax.dot_general(
            inverses[p], permuter, (((1,), (1,)), ((), ())), preferred_element_type=F32
        ).astype(BF16)

    for side in range(2):
        present = me_c > 0 if side == 0 else me_c < C - 1
        tile = left_tile if side == 0 else right_tile
        keep = lane >= 128 - MARGIN if side == 0 else lane < MARGIN

        @pl.when(present)
        def _():
            remote(
                hcol.at[side], hcol.at[2 + side], hcol_send.at[side], hcol_recv.at[side],
                me_r, me_c,
            ).wait_recv()
            got = hcol[2 + side]
            S[span, tile] = jnp.where(keep, got, 0.0)
            Wt[span, tile] = jnp.where(keep, pltpu.roll(got, 8 if side == 0 else 120, 1), 0.0)

        @pl.when(jnp.logical_not(present))
        def _():
            S[span, tile] = jnp.zeros((tall, 128), F32)
            Wt[span, tile] = jnp.zeros((tall, 128), F32)

    breadth = S.shape[1]

    def beside(ref, base):
        block = ref[pl.ds(pl.multiple_of(base - 8, 8), 32), :]
        above = pltpu.roll(block, 1, 0)[8:24]
        below = pltpu.roll(block, 31, 0)[8:24]
        middle_rows = block[8:24]
        return (
            above
            + below
            + pltpu.roll(middle_rows, breadth - 1, 1)
            + pltpu.roll(middle_rows, 1, 1)
        )

    E1[pl.ds(0, 8), :] = edge_zero
    E1[pl.ds(own_x + 24, 8), :] = edge_zero

    def first_sweep(i, carry):
        base = pl.multiple_of(8 + i * 16, 8)
        here = pl.ds(base, 16)
        E1[here, :] = S[here, :] + Wt[here, :] * beside(S, base)
        return carry

    lax.fori_loop(0, tall // 16, first_sweep, 0)

    def second_sweep(i, carry):
        base = pl.multiple_of(16 + i * 16, 16)
        here = pl.ds(base, 16)
        final = S[here, :] + Wt[here, :] * beside(E1, base)
        smoothed[pl.ds(pl.multiple_of(i * 16, 16), 16), :] = final[:, 128 : 128 + own_y]
        return carry

    lax.fori_loop(0, own_x // 16, second_sweep, 0)

    for i in range(1, C):
        remote(
            st1.at[0], r1.at[lax.rem(me_c + C - i, C)], a1_send.at[i], a1_recv.at[i], me_r, me_c
        ).wait_recv()

    def a2_copy(i):
        row = lax.rem(me_r + i, R)
        return remote(
            r1.at[:, row], r2.at[pl.ds(me_r * C, C)], a2_send.at[i], a2_recv.at[i], row, me_c
        )

    for i in range(1, R):
        a2_copy(i).start()
    for c in range(C):
        r2[me_r * C + c] = r1[c, me_r]

    for k in range(chunks):
        for way in range(2):
            tops_arrive(way, 0, k)
            if R > 2:
                tops_start(way, 1, k)

    for i in range(1, R):
        remote(
            r1.at[:, 0], r2.at[pl.ds(lax.rem(me_r + R - i, R) * C, C)], a2_send.at[i],
            a2_recv.at[i], me_r, me_c,
        ).wait_recv()

    unknown = lax.broadcasted_iota(jnp.int32, (COARSE_DEV, 128), 0)

    def add_rows(i, total):
        rows = slots[pl.ds(pl.multiple_of(i * 8, 8), 8), :]
        for j in range(8):
            total = total + jnp.where(unknown == rows[j : j + 1, :], r2[i * 8 + j], 0.0)
        return total

    total = lax.fori_loop(0, owners // 8, add_rows, jnp.zeros((COARSE_DEV, 128), F32))
    coarse[...] = jnp.sum(jnp.transpose(total), axis=0, keepdims=True)

    for t in range(1, len(orders[0])):
        for p in range(2):
            low_forward(p, t)
    for copy in load_low + load_tops:
        copy.wait()
    load_trailing.wait()
    for d in range(1, R - 2):
        for k in range(chunks):
            for way in range(2):
                tops_arrive(way, d, k)
                tops_start(way, d + 1, k)

    tile_rows = lb.shape[2]
    upd_copies, upp_copies = [], []
    for k in range(chunks):
        if R > 2:
            for way in range(2):
                tops_arrive(way, R - 2, k)
        columns = pl.ds(k * CHUNK, CHUNK)
        one = jnp.dot(maps[0], tb[k, 0], preferred_element_type=F32).astype(BF16)
        up[0, :, columns] = one
        two = (
            tb[k, 1].astype(F32) - jnp.dot(link[...], one, preferred_element_type=F32)
        ).astype(BF16)
        up[1, :, columns] = jnp.dot(maps[1], two, preferred_element_type=F32).astype(BF16)
        copy = pltpu.make_async_copy(
            up.at[:, :, columns], upper.at[:, :, columns], upp_sem.at[k]
        )
        copy.start()
        upp_copies.append(copy)

        def apply(i, carry):
            rows = pl.ds(pl.multiple_of(i * tile_rows, tile_rows), tile_rows)
            tr[rows, columns] = (
                tr[rows, columns].astype(F32)
                - jnp.dot(lb[0, i], up[0, :, columns], preferred_element_type=F32)
                - jnp.dot(lb[1, i], up[1, :, columns], preferred_element_type=F32)
            ).astype(BF16)
            return carry

        lax.fori_loop(0, C, apply, 0)
        copy = pltpu.make_async_copy(tr.at[:, columns], updated.at[:, columns], upd_sem.at[k])
        copy.start()
        upd_copies.append(copy)

    for d in range(R - 1):
        for k in range(chunks):
            for way in range(2):

                @pl.when(tops_sends(way, d))
                def _():
                    tops_copy(way, d, k).wait_send()

    for p in range(2):
        for t, bit in enumerate(orders[p]):
            for m in masks_of(orders[p][:t]):
                low_copy(p, m, bit).wait_send()
    for side, present in enumerate((me_r > 0, me_r < R - 1)):

        @pl.when(present)
        def _():
            row_copy(side).wait_send()

    for side, present in enumerate((me_c > 0, me_c < C - 1)):

        @pl.when(present)
        def _():
            col_copy(side).wait_send()

    for i in range(1, C):
        a1_copy(i).wait_send()
    for i in range(1, R):
        a2_copy(i).wait_send()
    for copy in upp_copies + upd_copies:
        copy.wait()


def shards(R, C, trailing, low_factor, panel_tops, diag_inverses, link_rows, pivots, residual,
           diagonal, coupling, basis_cells, basis_weights, coarse_slots):
    rows, columns = trailing.shape
    panel = diag_inverses.shape[1]
    own_x, own_y = residual.shape
    chunks = columns // CHUNK
    devices = R * C
    any_spec = pl.BlockSpec(memory_space=pl.ANY)
    vmem = pl.BlockSpec(memory_space=pltpu.VMEM)
    dma = pltpu.SemaphoreType.DMA
    updated, upper_rows, smoothed, coarse = pl.pallas_call(
        functools.partial(kernel, R, C),
        out_shape=(
            jax.ShapeDtypeStruct((rows, columns), BF16),
            jax.ShapeDtypeStruct((2, panel, columns), BF16),
            jax.ShapeDtypeStruct((own_x, own_y), F32),
            jax.ShapeDtypeStruct((1, COARSE_DEV), F32),
        ),
        in_specs=[any_spec] * 3 + [vmem] * 9,
        out_specs=(any_spec, any_spec, vmem, vmem),
        scratch_shapes=[
            pltpu.VMEM((chunks, 2, panel, CHUNK), BF16),
            pltpu.VMEM((2, C, low_factor.shape[1], panel), BF16),
            pltpu.VMEM((rows, columns), BF16),
            pltpu.VMEM((2, panel, columns), BF16),
            pltpu.VMEM((2, panel, panel), BF16),
            pltpu.VMEM((own_x + 32, own_y + 256), F32),
            pltpu.VMEM((own_x + 32, own_y + 256), F32),
            pltpu.VMEM((own_x + 32, own_y + 256), F32),
            pltpu.VMEM((2, 2, 8, own_y), F32),
            pltpu.VMEM((2, 2, 8, own_y), F32),
            pltpu.VMEM((4, own_x + 16, 128), F32),
            pltpu.VMEM((3 * own_x, own_y), BF16),
            pltpu.VMEM((C, R, 1, 128), F32),
            pltpu.VMEM((C, R, 1, 128), F32),
            pltpu.VMEM((devices, 1, 128), F32),
            dma((2, R - 1, chunks)),
            dma((2, R - 1, chunks)),
            dma((2, C)),
            dma((2, C)),
            dma((2,)),
            dma((2,)),
            dma((2,)),
            dma((2,)),
            dma((C,)),
            dma((C,)),
            dma((R,)),
            dma((R,)),
            dma((3,)),
            dma((chunks,)),
            dma((chunks,)),
            dma((chunks,)),
        ],
        compiler_params=pltpu.CompilerParams(
            collective_id=0, has_side_effects=True, vmem_limit_bytes=56 * 1024 * 1024
        ),
        cost_estimate=pl.CostEstimate(
            flops=2 * rows * columns * 2 * panel, bytes_accessed=4 * rows * columns,
            transcendentals=0,
        ),
    )(
        trailing, low_factor, panel_tops, diag_inverses, link_rows, pivots, residual, diagonal,
        coupling, basis_cells[0], basis_weights[0], coarse_slots[0],
    )
    return updated, upper_rows, smoothed, coarse.reshape(-1)


def solution(mesh):
    return jax.shard_map(
        functools.partial(shards, mesh.shape["row"], mesh.shape["col"]),
        mesh=mesh,
        in_specs=(
            P("row", "col"),
            P(None, ("row", "col"), None),
            P(None, "row", "col"),
            P(),
            P(),
            P(),
            P("row", "col"),
            P("row", "col"),
            P("row", "col"),
            P(("row", "col"), None, None),
            P(("row", "col"), None, None),
            P(("row", "col"), None, None),
        ),
        out_specs=(P("row", "col"), P(None, None, "col"), P("row", "col"), P(("row", "col"))),
        check_vma=False,
    )
```

time: 148 us -> 89.6 us (0.61)
  Pallas kernels: 0 us -> 79 us
  waiting for transfers between devices: 47.2 us -> 0 us
  matrix products: 37.3 us -> 0 us
  starting transfers between devices: 18.6 us -> 0 us
  between operations: 14.4 us -> 0.65 us
  local copies, waits for them, and re-layouts: 18.7 us -> 8.51 us
  other arithmetic: 10.5 us -> 1.27 us
    pallas_call x0 -> x1, Pallas kernels: none -> 79 us  [shards(): pl.pallas_call(functools.partial(kernel, R, C), out_shape=(jax.ShapeDtype...]
    all_gather x2 -> x0, waiting for transfers between devices: 45.3 us -> none  [the longest x1 23.2 us: shards(): pieces = lax.all_gather(low_factor, 'col', axis=1, tiled=True)]
    dot_general x9 -> x0, matrix products: 37.3 us -> none  [the longest x1 10.1 us: shards(): jnp.dot(pieces[1], upper_rows[1], preferred_element_type=jnp.float32)]
    ppermute x4 -> x0, starting transfers between devices: 11 us -> none  [the longest x2 7.56 us: with_halo(): lax.ppermute(tail, axis, [(i, (i + 1) % count) for i in range(ends)])]
    unnamed x22 -> x7, local copies, waits for them, and re-layouts: 17.3 us -> 8.51 us
    all_to_all x1 -> x0, starting transfers between devices: 7.61 us -> none  [shards(): lax.all_to_all(outgoing, ('row', 'col'), split_axis=0, concat_axis=0, til...]
    another operation x1 -> x0, other arithmetic: 3.36 us -> none  [solve_panels(): return jnp.stack([upper_one, upper_two])]
    add x2 -> x0, other arithmetic: 2.38 us -> none  [sweeps(): solution = source + weight * beside]
  transfers between devices with their start and end apart: 7 -> 0, of which waited for: 3 -> 0; matrix products, arithmetic and copies ran while one was open for 27% -> 0% of each run, Pallas kernels for 0% -> 0%
where the time goes in v1:
time: 89.6 us; the launch traced here: 89.5 us
  Pallas kernels  79 us (88%)
  local copies, waits for them, and re-layouts  8.51 us (9%)
  other arithmetic  1.27 us (1%)
    pallas_call x1, Pallas kernels, shards(): pl.pallas_call(functools.partial(kernel, R, C), out_shape=(jax.ShapeDtype...  79 us
    unnamed x7, local copies, waits for them, and re-layouts  8.51 us

profile of v1, /device:TPU:1, one launch (start us, length us, event | category | flops | bytes accessed | tf_op | source)
XLA Modules:
  0.0 89.5 jit_solution(15905530021258912606)
XLA Ops:
  0.6 79.0 %shard_map.147 = (bf16[2048,1536]{1,0:T(8,128)(2,1)}, bf16[2,512,1536]{2,1,0:T(8,128)(2,1)}, f32[256,512]{1,0:T(8,128)}, f32[1,384]{1,0:T(1,128)}) custom-call(bf16[2048,1536]{1,0:T(8,128)(2,1)} %trailing.1, bf16[2,256,512]{2,1,0:T(8,128)(2,1)} %low.1, bf16[2,128,1536]{2,1,0:T(8,128)(2,1)} %tops.1, bf16[2,512,512]{2,1,0:T(8,128)(2,1)} %inverses.1, ...), custom_call_target="tpu_custom_call" | custom-call | flops 6442450944 | bytes 12582912 | tf_op jit(solution)/shard_map/pallas_call | solution.py:503
  79.7 1.3 %reduce = f32[384]{0:T(512)} reduce(f32[1,384]{1,0:T(1,128)} %get-tuple-element.11, f32[]{:T(128)} %constant.3), dimensions={0}, to_apply=%get-tuple-element.11.reduce_sub_computation | reduce | bytes 3076 | tf_op jit(solution)/shard_map/pallas_call | solution.py:503
  80.9 0.0 copy-start
  80.9 6.0 %copy.19 = bf16[2048,1536]{1,0:T(8,128)(2,1)} copy(bf16[2048,1536]{1,0:T(8,128)(2,1)} %get-tuple-element.16) | data formatting | bytes 12582912
  87.0 0.0 copy-done
  87.0 0.0 copy-start.1
  87.0 1.7 %copy.20 = bf16[2,512,1536]{2,1,0:T(8,128)(2,1)} copy(bf16[2,512,1536]{2,1,0:T(8,128)(2,1)S(1)} %copy-done) | data formatting | bytes 6291456
  88.7 0.0 copy-done.1
  88.7 0.8 copy.21
Async XLA Ops:
  80.9 6.1 %copy-start = (bf16[2,512,1536]{2,1,0:T(8,128)(2,1)S(1)}, bf16[2,512,1536]{2,1,0:T(8,128)(2,1)}, u32[]{:S(2)}) copy-start(bf16[2,512,1536]{2,1,0:T(8,128)(2,1)} %get-tuple-element.17) | copy-start | bytes 9437188
  87.0 1.7 %copy-start.1 = (f32[256,512]{1,0:T(8,128)S(1)}, f32[256,512]{1,0:T(8,128)}, u32[]{:S(2)}) copy-start(f32[256,512]{1,0:T(8,128)} %get-tuple-element.18) | copy-start | bytes 1572868

commit v2 on v1

--- a/solution.py
+++ b/solution.py
@@ -10,7 +10,8 @@
 MARGIN = 3
 COARSE_DEV = 384
 CHUNK = 256
-ROW_TILE = 512
+PARTS = 8
+ROW_TILE = 1024
 MESH = pl.DeviceIdType.MESH
 F32 = jnp.float32
 BF16 = jnp.bfloat16
@@ -44,6 +45,19 @@
     trailing,
     low,
     tops,
+    inverses_in,
+    link_in,
+    pivots_in,
+    residual_in,
+    diagonal_in,
+    coupling_in,
+    cells_in,
+    weights_in,
+    slots_in,
+    updated,
+    upper,
+    smoothed_out,
+    coarse_out,
     inverses,
     link,
     pivots,
@@ -53,8 +67,6 @@
     cells,
     weights,
     slots,
-    updated,
-    upper,
     smoothed,
     coarse,
     tb,
@@ -88,6 +100,8 @@
     tops_load,
     upd_sem,
     upp_sem,
+    small_sem,
+    out_sem,
 ):
     me_r, me_c = lax.axis_index("row"), lax.axis_index("col")
     chunks = tb.shape[0]
@@ -115,7 +129,24 @@
             barrier, inc=1, device_id=(me_r, lax.rem(me_c + i, C)), device_id_type=MESH
         )
 
-    load_trailing = pltpu.make_async_copy(trailing, tr, load_sem.at[0])
+    ready = updated.shape[1]
+    load_trailing = pltpu.make_async_copy(trailing.at[:, pl.ds(0, ready)], tr, load_sem.at[0])
+    small = [
+        pltpu.make_async_copy(source, target, small_sem.at[i])
+        for i, (source, target) in enumerate(
+            (
+                (residual_in, residual),
+                (diagonal_in, diagonal),
+                (coupling_in, coupling),
+                (cells_in, cells),
+                (weights_in, weights),
+                (inverses_in, inverses),
+                (pivots_in, pivots),
+                (slots_in, slots),
+                (link_in, link),
+            )
+        )
+    ]
     load_low = [
         pltpu.make_async_copy(low.at[p], lb.at[p, me_c], load_sem.at[1 + p]) for p in range(2)
     ]
@@ -180,6 +211,8 @@
             for bit in order[t + 1 :]:
                 low_copy(p, arrived, bit).start()
 
+    for copy in small[:5]:
+        copy.start()
     pl.semaphore_wait(barrier, R - 1 + C - 1)
     for k in range(chunks):
         for way in range(2):
@@ -187,10 +220,12 @@
     for t in range(len(orders[0])):
         for p in range(2):
             low_copy(p, 0, orders[p][t]).start()
-    for copy in load_tops + load_low:
+    for copy in small[5:] + load_tops + load_low:
         copy.start()
     load_trailing.start()
 
+    for copy in small[:3]:
+        copy.wait()
     mid_y = pl.ds(128, own_y)
     src_own = residual[...] * (1.0 / diagonal[...])
     S[pl.ds(16, own_x), mid_y] = src_own
@@ -246,6 +281,8 @@
             )
         return carry
 
+    for copy in small[3:5]:
+        copy.wait()
     lax.fori_loop(0, owners // 8, pick, 0)
 
     def a1_copy(i):
@@ -260,6 +297,18 @@
 
     for p in range(2):
         low_forward(p, 0)
+
+    passed = [0]
+
+    def tops_pass(number):
+        for k in range(passed[0], min(passed[0] + number, chunks)):
+            for way in range(2):
+                tops_arrive(way, 0, k)
+                if R > 2:
+                    tops_start(way, 1, k)
+        passed[0] = min(passed[0] + number, chunks)
+
+    tops_pass(1)
 
     row_at = lax.broadcasted_iota(jnp.int32, (8, own_y), 0)
     edge_zero = jnp.zeros((8, S.shape[1]), F32)
@@ -311,6 +360,10 @@
     def _():
         col_copy(1).start()
 
+    tops_pass(2)
+
+    for copy in small[5:7]:
+        copy.wait()
     count = inverses.shape[1]
     for p in range(2):
         permuter = (
@@ -373,6 +426,8 @@
         return carry
 
     lax.fori_loop(0, own_x // 16, second_sweep, 0)
+    outs = [pltpu.make_async_copy(smoothed, smoothed_out, out_sem.at[0])]
+    outs[0].start()
 
     for i in range(1, C):
         remote(
@@ -390,11 +445,7 @@
     for c in range(C):
         r2[me_r * C + c] = r1[c, me_r]
 
-    for k in range(chunks):
-        for way in range(2):
-            tops_arrive(way, 0, k)
-            if R > 2:
-                tops_start(way, 1, k)
+    tops_pass(chunks)
 
     for i in range(1, R):
         remote(
@@ -402,6 +453,7 @@
             a2_recv.at[i], me_r, me_c,
         ).wait_recv()
 
+    small[7].wait()
     unknown = lax.broadcasted_iota(jnp.int32, (COARSE_DEV, 128), 0)
 
     def add_rows(i, total):
@@ -412,6 +464,8 @@
 
     total = lax.fori_loop(0, owners // 8, add_rows, jnp.zeros((COARSE_DEV, 128), F32))
     coarse[...] = jnp.sum(jnp.transpose(total), axis=0, keepdims=True)
+    outs.append(pltpu.make_async_copy(coarse, coarse_out, out_sem.at[1]))
+    outs[1].start()
 
     for t in range(1, len(orders[0])):
         for p in range(2):
@@ -419,13 +473,17 @@
     for copy in load_low + load_tops:
         copy.wait()
     load_trailing.wait()
+    small[8].wait()
     for d in range(1, R - 2):
         for k in range(chunks):
             for way in range(2):
                 tops_arrive(way, d, k)
                 tops_start(way, d + 1, k)
 
-    tile_rows = lb.shape[2]
+    held = lb.shape[2]
+    tile_rows = min(ROW_TILE, tr.shape[0])
+    group = tile_rows // held
+    depth = lb.shape[3]
     upd_copies, upp_copies = [], []
     for k in range(chunks):
         if R > 2:
@@ -444,16 +502,26 @@
         copy.start()
         upp_copies.append(copy)
 
+
         def apply(i, carry):
             rows = pl.ds(pl.multiple_of(i * tile_rows, tile_rows), tile_rows)
+            blocks = pl.ds(i * group, group)
             tr[rows, columns] = (
                 tr[rows, columns].astype(F32)
-                - jnp.dot(lb[0, i], up[0, :, columns], preferred_element_type=F32)
-                - jnp.dot(lb[1, i], up[1, :, columns], preferred_element_type=F32)
+                - jnp.dot(
+                    lb[0, blocks].reshape(tile_rows, depth),
+                    up[0, :, columns],
+                    preferred_element_type=F32,
+                )
+                - jnp.dot(
+                    lb[1, blocks].reshape(tile_rows, depth),
+                    up[1, :, columns],
+                    preferred_element_type=F32,
+                )
             ).astype(BF16)
             return carry
 
-        lax.fori_loop(0, C, apply, 0)
+        lax.fori_loop(0, tr.shape[0] // tile_rows, apply, 0)
         copy = pltpu.make_async_copy(tr.at[:, columns], updated.at[:, columns], upd_sem.at[k])
         copy.start()
         upd_copies.append(copy)
@@ -486,8 +554,37 @@
         a1_copy(i).wait_send()
     for i in range(1, R):
         a2_copy(i).wait_send()
-    for copy in upp_copies + upd_copies:
+    for copy in upp_copies + upd_copies + outs:
         copy.wait()
+
+
+def finish(
+    partial, upper_in, smoothed_in, coarse_in,
+    updated, upper, smoothed, coarse,
+    pv, uv, sv, load_sem, copy_sem,
+):
+    part = partial.shape[0] // PARTS
+    pieces = [
+        (partial.at[here], pv.at[here], updated.at[here])
+        for here in (pl.ds(i * part, part) for i in range(PARTS))
+    ]
+    pieces += [(upper_in.at[p], uv.at[p], upper.at[p]) for p in range(2)]
+    pieces.append((smoothed_in, sv, smoothed))
+    moves = [
+        (
+            pltpu.make_async_copy(source, through, load_sem.at[i]),
+            pltpu.make_async_copy(through, target, copy_sem.at[i]),
+        )
+        for i, (source, through, target) in enumerate(pieces)
+    ]
+    for load, _ in moves:
+        load.start()
+    coarse[...] = coarse_in[0, :]
+    for load, store in moves:
+        load.wait()
+        store.start()
+    for _, store in moves:
+        store.wait()
 
 
 def shards(R, C, trailing, low_factor, panel_tops, diag_inverses, link_rows, pivots, residual,
@@ -500,20 +597,33 @@
     any_spec = pl.BlockSpec(memory_space=pl.ANY)
     vmem = pl.BlockSpec(memory_space=pltpu.VMEM)
     dma = pltpu.SemaphoreType.DMA
-    updated, upper_rows, smoothed, coarse = pl.pallas_call(
+    ready = columns
+    held_shape = (2, C, low_factor.shape[1], panel)
+    partial, upper_in, smoothed_in, coarse_in = pl.pallas_call(
         functools.partial(kernel, R, C),
         out_shape=(
-            jax.ShapeDtypeStruct((rows, columns), BF16),
+            jax.ShapeDtypeStruct((rows, ready), BF16),
             jax.ShapeDtypeStruct((2, panel, columns), BF16),
             jax.ShapeDtypeStruct((own_x, own_y), F32),
             jax.ShapeDtypeStruct((1, COARSE_DEV), F32),
         ),
-        in_specs=[any_spec] * 3 + [vmem] * 9,
-        out_specs=(any_spec, any_spec, vmem, vmem),
+        in_specs=[any_spec] * 12,
+        out_specs=[any_spec] * 4,
         scratch_shapes=[
+            pltpu.VMEM((2, panel, panel), BF16),
+            pltpu.VMEM((panel, panel), BF16),
+            pltpu.VMEM(pivots.shape, jnp.int32),
+            pltpu.VMEM((own_x, own_y), F32),
+            pltpu.VMEM((own_x, own_y), F32),
+            pltpu.VMEM((own_x, own_y), F32),
+            pltpu.VMEM(basis_cells.shape[1:], jnp.int32),
+            pltpu.VMEM(basis_cells.shape[1:], F32),
+            pltpu.VMEM(basis_cells.shape[1:], jnp.int32),
+            pltpu.VMEM((own_x, own_y), F32),
+            pltpu.VMEM((1, COARSE_DEV), F32),
             pltpu.VMEM((chunks, 2, panel, CHUNK), BF16),
-            pltpu.VMEM((2, C, low_factor.shape[1], panel), BF16),
-            pltpu.VMEM((rows, columns), BF16),
+            pltpu.VMEM(held_shape, BF16),
+            pltpu.VMEM((rows, ready), BF16),
             pltpu.VMEM((2, panel, columns), BF16),
             pltpu.VMEM((2, panel, panel), BF16),
             pltpu.VMEM((own_x + 32, own_y + 256), F32),
@@ -542,6 +652,8 @@
             dma((chunks,)),
             dma((chunks,)),
             dma((chunks,)),
+            dma((9,)),
+            dma((2,)),
         ],
         compiler_params=pltpu.CompilerParams(
             collective_id=0, has_side_effects=True, vmem_limit_bytes=56 * 1024 * 1024
@@ -554,7 +666,26 @@
         trailing, low_factor, panel_tops, diag_inverses, link_rows, pivots, residual, diagonal,
         coupling, basis_cells[0], basis_weights[0], coarse_slots[0],
     )
-    return updated, upper_rows, smoothed, coarse.reshape(-1)
+    updated, upper_rows, smoothed, coarse = pl.pallas_call(
+        finish,
+        out_shape=(
+            jax.ShapeDtypeStruct((rows, columns), BF16),
+            jax.ShapeDtypeStruct((2, panel, columns), BF16),
+            jax.ShapeDtypeStruct((own_x, own_y), F32),
+            jax.ShapeDtypeStruct((COARSE_DEV,), F32),
+        ),
+        in_specs=[any_spec] * 3 + [vmem],
+        out_specs=[any_spec] * 3 + [vmem],
+        scratch_shapes=[
+            pltpu.VMEM((rows, ready), BF16),
+            pltpu.VMEM((2, panel, columns), BF16),
+            pltpu.VMEM((own_x, own_y), F32),
+            dma((PARTS + 3,)),
+            dma((PARTS + 3,)),
+        ],
+        compiler_params=pltpu.CompilerParams(vmem_limit_bytes=56 * 1024 * 1024),
+    )(partial, upper_in, smoothed_in, coarse_in)
+    return updated, upper_rows, smoothed, coarse
 
 
 def solution(mesh):

time: 89.6 us -> 72.7 us (0.81)
  local copies, waits for them, and re-layouts: 8.51 us -> 0 us
  Pallas kernels: 79 us -> 71.5 us
  other arithmetic: 1.27 us -> 0 us
    pallas_call x1, Pallas kernels: 79 us -> 62.8 us  [shards(): pl.pallas_call(functools.partial(kernel, R, C), out_shape=(jax.ShapeDtype...]
    pallas_call x0 -> x1, Pallas kernels: none -> 8.68 us  [shards(): pl.pallas_call(finish, out_shape=(jax.ShapeDtypeStruct((rows, columns), B...]
    unnamed x7 -> x0, local copies, waits for them, and re-layouts: 8.51 us -> none
    pallas_call x1 -> x0, other arithmetic: 1.27 us -> none  [shards(): pl.pallas_call(functools.partial(kernel, R, C), out_shape=(jax.ShapeDtype...]
where the time goes in v2:
time: 72.7 us; the launch traced here: 72.2 us
  Pallas kernels  71.5 us (98%)
    pallas_call x1, Pallas kernels, shards(): pl.pallas_call(functools.partial(kernel, R, C), out_shape=(jax.ShapeDtype...  62.8 us
    pallas_call x1, Pallas kernels, shards(): pl.pallas_call(finish, out_shape=(jax.ShapeDtypeStruct((rows, columns), B...  8.68 us

profile of v2, /device:TPU:1, one launch (start us, length us, event | category | flops | bytes accessed | tf_op | source)
XLA Modules:
  0.0 72.2 jit_solution(11968583248432846159)
XLA Ops:
  0.6 62.8 %shard_map.147 = (bf16[2048,1536]{1,0:T(8,128)(2,1)}, bf16[2,512,1536]{2,1,0:T(8,128)(2,1)}, f32[256,512]{1,0:T(8,128)}, f32[1,384]{1,0:T(1,128)}) custom-call(bf16[2048,1536]{1,0:T(8,128)(2,1)} %trailing.1, bf16[2,256,512]{2,1,0:T(8,128)(2,1)} %low.1, bf16[2,128,1536]{2,1,0:T(8,128)(2,1)} %tops.1, bf16[2,512,512]{2,1,0:T(8,128)(2,1)} %inverses_in.1, ...), custom_call_target="tpu_custom_call" | custom-call | flops 6442450944 | bytes 12582912 | tf_op jit(solution)/shard_map/pallas_call | solution.py:602
  63.5 8.7 %shard_map.148 = (bf16[2048,1536]{1,0:T(8,128)(2,1)}, bf16[2,512,1536]{2,1,0:T(8,128)(2,1)}, f32[256,512]{1,0:T(8,128)}, f32[384]{0:T(512)}) custom-call(bf16[2048,1536]{1,0:T(8,128)(2,1)} %get-tuple-element.8.partial, bf16[2,512,1536]{2,1,0:T(8,128)(2,1)} %get-tuple-element.9.upper_in, f32[256,512]{1,0:T(8,128)} %get-tuple-element.10.smoothed_in, ...), custom_call_target="tpu_custom_call" | custom-call | tf_op jit(solution)/shard_map/pallas_call | solution.py:669
